TPU v7x, 512 devices: a whole 4x4x16 slice. The times are simulated.
512 devices in a mesh: occ: 16 (over y_lo, x, core), vir: 32 (over z, y_hi).
Axes of the slice: x: 4, y: 4 (y_hi: 2, y_lo: 2; y = y_hi * 2 + y_lo), z: 16, core: 2. Of those that a mesh axis runs over, the one named last changes fastest.
Arguments:
- factor: float32 [16, 4096, 1280], P('occ', 'vir'), may hold values from -0.6 to 0.6
- occ_energy: float32 [16], P('occ'), may hold values from -2 to -0.5
- vir_energy: float32 [4096], P('vir'), may hold values from 0.2 to 4.7
Outputs:
- aux_density: float32 [16, 4096, 1280], P('occ', 'vir')
- pair_trace: float32 [16, 3], P('occ')
All inputs are finite; a program needn't handle non-finite values.
Results may differ from a plain program's by a relative error of at most 0.00013.
Values sent between devices are 32-bit elements; how exact they have to be, the bound alone decides.
A program may use at most 64 MiB of HBM per device.

v0:
```python
import jax
import jax.numpy as jnp
from jax import lax
from jax.sharding import PartitionSpec as P

NVIR = 4096
STEPS = 3


def passed_along(block, axis, distance):
    devices = range(lax.axis_size(axis))
    route = [((i - distance) % len(devices), i) for i in devices]
    return lax.ppermute(block, axis, route)


def partner(value, axis, apart):
    return lax.ppermute(value, axis, [(i, i ^ 1 << apart) for i in range(lax.axis_size(axis))])


def contract(pattern, former, latter):
    return jnp.einsum(
        pattern, former, latter, precision=lax.Precision.HIGHEST, preferred_element_type=jnp.float32
    )


def local(factor, occ_energy, vir_energy):
    cycle_rows = factor
    cycle_occ = occ_energy
    density = jnp.zeros(factor.shape, jnp.float32)
    carried = jnp.zeros(factor.shape, jnp.float32)
    traces = []
    for offset in range(STEPS):
        if offset > 0:
            cycle_rows, cycle_occ, carried = passed_along(
                (cycle_rows, cycle_occ, carried), "occ", 1
            )
        far_rows, far_vir = partner((cycle_rows, vir_energy), "vir", 0)
        pair_occ = occ_energy[:, None] + cycle_occ[None, :]
        gap_diag = (
            pair_occ[:, :, None, None]
            - vir_energy[None, None, :, None]
            - vir_energy[None, None, None, :]
        )
        gap_off = (
            pair_occ[:, :, None, None]
            - vir_energy[None, None, :, None]
            - far_vir[None, None, None, :]
        )
        k_diag = contract("iap,jbp->ijab", factor, cycle_rows)
        k_off = contract("iap,jbp->ijab", factor, far_rows)
        amp_diag = k_diag / gap_diag
        amp_off = k_off / gap_off
        bar_diag = 2.0 * amp_diag - jnp.swapaxes(amp_diag, 2, 3)
        k_cross = jnp.swapaxes(partner(k_off, "vir", 0), 2, 3)
        amp_cross = k_cross / gap_off
        bar_off = 2.0 * amp_off - amp_cross
        traces.append(jnp.sum(amp_diag * bar_diag + amp_off * bar_off, axis=(2, 3)) / NVIR)
        density = (
            density
            + contract("ijab,jbp->iap", bar_diag, cycle_rows)
            + contract("ijab,jbp->iap", bar_off, far_rows)
        )
        returned = contract("ijab,iap->jbp", bar_diag, factor)
        returned = returned + partner(contract("ijab,iap->jbp", bar_off, factor), "vir", 0)
        carried = carried + returned
    density = density + passed_along(carried, "occ", 1 - STEPS)
    pair_trace = lax.psum(jnp.concatenate(traces, axis=1), "vir")
    return (density, pair_trace)


def solution(mesh):
    placed = (P("occ", "vir", None), P("occ"), P("vir"))
    return jax.shard_map(
        local,
        mesh=mesh,
        in_specs=placed,
        out_specs=(P("occ", "vir", None), P("occ", None)),
        check_vma=False,
    )
```

profile of v0, /device:TPU:2, one launch (start us, length us, event | category | flops | bytes accessed | tf_op | source)
XLA Modules:
  0.0 244.3 jit_solution(12219553187128201509)
XLA Ops:
  0.6 2.1 collective-permute-start.3
  2.7 5.1 %collective-permute-start = (f32[1,128,1280]{2,1,0:T(8,128)}, f32[1,128,1280]{2,1,0:T(8,128)S(1)}, u32[]{:S(2)}, u32[]{:S(2)}) collective-permute-start(f32[1,128,1280]{2,1,0:T(8,128)} %param.3), channel_id=1, source_target_pairs={{0,1},{1,0},{2,3},{3,2},{4,5},{5,4},{6,7},{7,6},{8,9},{9,8},{10,11... | collective-permute-start | bytes 1966088 | tf_op jit(solution)/shard_map/ppermute | solution.py:17
  7.8 3.2 %collective-permute-start.4 = (f32[1]{0:T(128)}, f32[1]{0:T(128)}, u32[]{:S(2)}, u32[]{:S(2)}) collective-permute-start(f32[1]{0:T(128)} %param.4), channel_id=1, source_target_pairs={{480,0},{0,32},{32,64},{64,96},{96,128},{128,160},{160,192},{192,2... | collective-permute-start | bytes 20 | tf_op jit(solution)/shard_map/ppermute | solution.py:13
  11.0 2.2 collective-permute-start.1
  14.0 1.9 collective-permute-start.8
  16.6 2.4 collective-permute-done.8
  19.7 1.2 broadcast_subtract_fusion.2
  20.9 0.7 broadcast_subtract_fusion.1
  21.7 2.0 fusion.6
  23.8 1.9 collective-permute-start.7
  25.8 1.6 fusion.31
  27.4 1.3 convolution_bitcast_fusion.10
  28.7 5.2 %collective-permute-start.2 = (f32[1,1,128,128]{2,3,0,1:T(8,128)}, f32[1,1,128,128]{2,3,0,1:T(8,128)}, u32[]{:S(2)}, u32[]{:S(2)}) collective-permute-start(f32[1,1,128,128]{2,3,0,1:T(8,128)} %convolution_bitcast_fusion.10), channel_id=1, source_target_pairs={{0,1},{1,0},{2,3},{3,2},{4,5},{5,4},{6,7},{7,6},{8,9},{9,8},{10,11... | collective-permute-start | bytes 196616 | tf_op jit(solution)/shard_map/ppermute | solution.py:17
  33.9 2.2 collective-permute-start.5
  36.2 0.7 fusion.7
  37.2 1.6 copy.9
  38.7 2.5 %convolution_bitcast_fusion.4 = f32[1,128,1280]{2,1,0:T(8,128)} fusion(f32[1,128,1280]{2,1,0:T(8,128)S(1)} %copy-done, f32[1,1,128,128]{2,3,0,1:T(8,128)} %copy.9, f32[128]{0:T(128)S(1)} %collective-permute-done.1, f32[128]{0:T(128)S(1)} %get-tuple-element.6, f32[1,1,128,128]{2,3,0,1:T(8,128)} %convolution_bitcast_fusion.10), kind=kOutput, calls=%fused_computation.13 | convolution fusion | flops 251740160 | bytes 1442816 | tf_op jit(solution)/shard_map/ijab,iap->jbp/dot_general | solution.py:21
  41.2 5.1 %collective-permute-start.11 = (f32[1,128,1280]{2,1,0:T(8,128)}, f32[1,128,1280]{2,1,0:T(8,128)}, u32[]{:S(2)}, u32[]{:S(2)}) collective-permute-start(f32[1,128,1280]{2,1,0:T(8,128)} %convolution_bitcast_fusion.4), channel_id=1, source_target_pairs={{0,1},{1,0},{2,3},{3,2},{4,5},{5,4},{6,7},{7,6},{8,9},{9,8},{10,11... | collective-permute-start | bytes 1966088 | tf_op jit(solution)/shard_map/ppermute | solution.py:17
  46.4 2.2 collective-permute-start.9
  48.6 1.6 convolution_add_fusion.3
  50.3 4.6 %collective-permute-done.5 = f32[1,128,1280]{2,1,0:T(8,128)S(1)} collective-permute-done((f32[1,128,1280]{2,1,0:T(8,128)S(1)}, f32[1,128,1280]{2,1,0:T(8,128)S(1)}, u32[]{:S(2)}, u32[]{:S(2)}) %collective-permute-start.5) | collective-permute-done | bytes 655392 | tf_op jit(solution)/shard_map/ppermute | solution.py:17
  55.6 2.2 collective-permute-start.6
  58.5 25.8 %collective-permute-done.6 = f32[1,1,128,128]{3,2,0,1:T(8,128)S(1)} collective-permute-done((f32[1,1,128,128]{3,2,0,1:T(8,128)S(1)}, f32[1,1,128,128]{3,2,0,1:T(8,128)S(1)}, u32[]{:S(2)}, u32[]{:S(2)}) %collective-permute-start.6) | collective-permute-done | bytes 65568 | tf_op jit(solution)/shard_map/ppermute | solution.py:17
  85.0 1.0 copy.15
  86.0 1.6 convolution_bitcast_fusion.2
  87.6 2.2 collective-permute-start.13
  89.9 1.8 convolution_bitcast_fusion.6
  91.7 5.1 %collective-permute-start.10 = (f32[1,1,128,128]{2,3,0,1:T(8,128)S(1)}, f32[1,1,128,128]{2,3,0,1:T(8,128)S(1)}, u32[]{:S(2)}, u32[]{:S(2)}) collective-permute-start(f32[1,1,128,128]{2,3,0,1:T(8,128)S(1)} %convolution_bitcast_fusion.6), channel_id=1, source_target_pairs={{0,1},{1,0},{2,3},{3,2},{4,5},{5,4},{6,7},{7,6},{8,9},{9,8},{10,11... | collective-permute-start | bytes 196616 | tf_op jit(solution)/shard_map/ppermute | solution.py:17
  96.8 2.6 %fusion.5 = f32[1,128,1280]{2,1,0:T(8,128)} fusion(f32[1,128,1280]{2,1,0:T(8,128)} %collective-permute-done.11, f32[1,128,1280]{2,1,0:T(8,128)S(1)} %copy-done, f32[1,1,128,128]{3,2,0,1:T(8,128)S(1)} %copy.6, f32[1,1,128,128]{2,3,0,1:T(8,128)S(1)} %fusion.6), kind=kOutput, calls=%fused_computation.15 | convolution fusion | flops 251854848 | bytes 2097152 | tf_op jit(solution)/shard_map/ijab,iap->jbp/dot_general | solution.py:21
  99.4 2.0 collective-permute-start.12
  101.4 7.9 %collective-permute-done.10 = f32[1,1,128,128]{2,3,0,1:T(8,128)S(1)} collective-permute-done((f32[1,1,128,128]{2,3,0,1:T(8,128)S(1)}, f32[1,1,128,128]{2,3,0,1:T(8,128)S(1)}, u32[]{:S(2)}, u32[]{:S(2)}) %collective-permute-start.10) | collective-permute-done | bytes 65568 | tf_op jit(solution)/shard_map/ppermute | solution.py:17
  109.4 0.7 broadcast_subtract_fusion
  110.3 1.6 convolution_bitcast_fusion
  111.8 2.2 collective-permute-start.15
  114.1 1.8 fusion.4
  115.9 2.0 add.74
  118.0 2.1 collective-permute-start.14
  120.1 1.5 add_reduce_fusion.2
  122.2 0.7 broadcast_multiply_fusion
  123.0 8.6 %collective-permute-done.15 = f32[1,128,1280]{2,1,0:T(8,128)} collective-permute-done((f32[1,128,1280]{2,1,0:T(8,128)}, f32[1,128,1280]{2,1,0:T(8,128)}, u32[]{:S(2)}, u32[]{:S(2)}) %collective-permute-start.15) | collective-permute-done | bytes 655392 | tf_op jit(solution)/shard_map/ppermute | solution.py:17
  131.6 1.8 fusion.3
  133.3 2.0 add.76
  135.3 7.2 %collective-permute-start.16 = (f32[1,128,1280]{2,1,0:T(8,128)}, f32[1,128,1280]{2,1,0:T(8,128)}, u32[]{:S(2)}, u32[]{:S(2)}) collective-permute-start(f32[1,128,1280]{2,1,0:T(8,128)} %add.76), channel_id=1, source_target_pairs={{64,0},{96,32},{128,64},{160,96},{192,128},{224,160},{256,192},{28... | collective-permute-start | bytes 1966088 | tf_op jit(solution)/shard_map/ppermute | solution.py:13
  142.6 0.7 fusion.11
  143.4 0.7 add_reduce_fusion
  145.4 0.7 fusion
  146.2 95.2 %psum.7 = f32[1,3]{1,0:T(1,128)} all-reduce(f32[1,3]{1,0:T(1,128)S(1)} %pad_maximum_fusion), channel_id=1, replica_groups=mesh['occ'=16,'vir'=32] {'vir'}, use_global_device_ids=true, to_apply=%region_3.0 | all-reduce | flops 3 | bytes 24 | tf_op jit(solution)/shard_map/psum | solution.py:67
  241.4 2.9 %fusion.2 = f32[1,128,1280]{2,1,0:T(8,128)} fusion(f32[1,128,1280]{2,1,0:T(8,128)} %collective-permute-done.16, f32[128,1280]{1,0:T(8,128)S(1)} %fusion, f32[1,128,1280]{2,1,0:T(8,128)} %collective-permute-done.9, f32[1,1,128,128]{2,3,0,1:T(8,128)S(1)} %copy.20, f32[1,1,128,128]{2,3,0,1:T(8,128)S(1)} %convolution_bitcast_fusion.6, ...), kind=kOutput, calls=%fused_computation.6 | convolution fusion | flops 252035072 | bytes 2818048 | tf_op jit(solution)/shard_map/ijab,jbp->iap/dot_general | solution.py:21
  (40 shorter events, 2.9 us)
Async XLA Ops:
  0.6 25.1 %copy-start = (f32[1,128,1280]{2,1,0:T(8,128)S(1)}, f32[1,128,1280]{2,1,0:T(8,128)}, u32[]{:S(2)}) copy-start(f32[1,128,1280]{2,1,0:T(8,128)} %param.3) | copy-start | bytes 1966084
  0.6 23.2 %collective-permute-start.3 = (f32[1,128,1280]{2,1,0:T(8,128)}, f32[1,128,1280]{2,1,0:T(8,128)S(1)}, u32[]{:S(2)}, u32[]{:S(2)}) collective-permute-start(f32[1,128,1280]{2,1,0:T(8,128)} %param.3), channel_id=1, source_target_pairs={{480,0},{0,32},{32,64},{64,96},{96,128},{128,160},{160,192},{192,2... | collective-permute-start | bytes 1966088 | tf_op jit(solution)/shard_map/ppermute | solution.py:13
  2.7 24.7 %collective-permute-start = (f32[1,128,1280]{2,1,0:T(8,128)}, f32[1,128,1280]{2,1,0:T(8,128)S(1)}, u32[]{:S(2)}, u32[]{:S(2)}) collective-permute-start(f32[1,128,1280]{2,1,0:T(8,128)} %param.3), channel_id=1, source_target_pairs={{0,1},{1,0},{2,3},{3,2},{4,5},{5,4},{6,7},{7,6},{8,9},{9,8},{10,11... | collective-permute-start | bytes 1966088 | tf_op jit(solution)/shard_map/ppermute | solution.py:17
  7.8 6.1 %collective-permute-start.4 = (f32[1]{0:T(128)}, f32[1]{0:T(128)}, u32[]{:S(2)}, u32[]{:S(2)}) collective-permute-start(f32[1]{0:T(128)} %param.4), channel_id=1, source_target_pairs={{480,0},{0,32},{32,64},{64,96},{96,128},{128,160},{160,192},{192,2... | collective-permute-start | bytes 20 | tf_op jit(solution)/shard_map/ppermute | solution.py:13
  11.0 27.7 %collective-permute-start.1 = (f32[128]{0:T(128)}, f32[128]{0:T(128)S(1)}, u32[]{:S(2)}, u32[]{:S(2)}) collective-permute-start(f32[128]{0:T(128)} %param.5), channel_id=1, source_target_pairs={{0,1},{1,0},{2,3},{3,2},{4,5},{5,4},{6,7},{7,6},{8,9},{9,8},{10,11... | collective-permute-start | bytes 1544 | tf_op jit(solution)/shard_map/ppermute | solution.py:17
  14.0 5.0 %collective-permute-start.8 = (f32[1]{0:T(128)}, f32[1]{0:T(128)}, u32[]{:S(2)}, u32[]{:S(2)}) collective-permute-start(f32[1]{0:T(128)} %collective-permute-done.4), channel_id=1, source_target_pairs={{480,0},{0,32},{32,64},{64,96},{96,128},{128,160},{160,192},{192,2... | collective-permute-start | bytes 20 | tf_op jit(solution)/shard_map/ppermute | solution.py:13
  23.8 22.5 %collective-permute-start.7 = (f32[1,128,1280]{2,1,0:T(8,128)S(1)}, f32[1,128,1280]{2,1,0:T(8,128)S(1)}, u32[]{:S(2)}, u32[]{:S(2)}) collective-permute-start(f32[1,128,1280]{2,1,0:T(8,128)S(1)} %collective-permute-done.3), channel_id=1, source_target_pairs={{480,0},{0,32},{32,64},{64,96},{96,128},{128,160},{160,192},{192,2... | collective-permute-start | bytes 1966088 | tf_op jit(solution)/shard_map/ppermute | solution.py:13
  28.7 7.5 %copy-start.7 = (f32[128]{0:T(128)S(1)}, f32[128]{0:T(128)}, u32[]{:S(2)}) copy-start(f32[128]{0:T(128)} %param.5) | copy-start | bytes 1540
  28.7 8.5 %collective-permute-start.2 = (f32[1,1,128,128]{2,3,0,1:T(8,128)}, f32[1,1,128,128]{2,3,0,1:T(8,128)}, u32[]{:S(2)}, u32[]{:S(2)}) collective-permute-start(f32[1,1,128,128]{2,3,0,1:T(8,128)} %convolution_bitcast_fusion.10), channel_id=1, source_target_pairs={{0,1},{1,0},{2,3},{3,2},{4,5},{5,4},{6,7},{7,6},{8,9},{9,8},{10,11... | collective-permute-start | bytes 196616 | tf_op jit(solution)/shard_map/ppermute | solution.py:17
  33.9 21.0 %collective-permute-start.5 = (f32[1,128,1280]{2,1,0:T(8,128)S(1)}, f32[1,128,1280]{2,1,0:T(8,128)S(1)}, u32[]{:S(2)}, u32[]{:S(2)}) collective-permute-start(f32[1,128,1280]{2,1,0:T(8,128)S(1)} %collective-permute-done.3), channel_id=1, source_target_pairs={{0,1},{1,0},{2,3},{3,2},{4,5},{5,4},{6,7},{7,6},{8,9},{9,8},{10,11... | collective-permute-start | bytes 1966088 | tf_op jit(solution)/shard_map/ppermute | solution.py:17
  38.7 9.9 %copy-start.1 = (f32[128,1280]{1,0:T(8,128)S(1)}, f32[128,1280]{1,0:T(8,128)}, u32[]{:S(2)}) copy-start(f32[128,1280]{1,0:T(8,128)} %fusion.31) | copy-start | bytes 1966084
  38.7 9.9 %copy-start.4 = (f32[1,1,128,128]{2,3,0,1:T(8,128)S(1)}, f32[1,1,128,128]{2,3,0,1:T(8,128)}, u32[]{:S(2)}) copy-start(f32[1,1,128,128]{2,3,0,1:T(8,128)} %copy.9) | copy-start | bytes 196612
  41.2 55.5 %collective-permute-start.11 = (f32[1,128,1280]{2,1,0:T(8,128)}, f32[1,128,1280]{2,1,0:T(8,128)}, u32[]{:S(2)}, u32[]{:S(2)}) collective-permute-start(f32[1,128,1280]{2,1,0:T(8,128)} %convolution_bitcast_fusion.4), channel_id=1, source_target_pairs={{0,1},{1,0},{2,3},{3,2},{4,5},{5,4},{6,7},{7,6},{8,9},{9,8},{10,11... | collective-permute-start | bytes 1966088 | tf_op jit(solution)/shard_map/ppermute | solution.py:17
  46.4 43.5 %collective-permute-start.9 = (f32[1,128,1280]{2,1,0:T(8,128)S(1)}, f32[1,128,1280]{2,1,0:T(8,128)}, u32[]{:S(2)}, u32[]{:S(2)}) collective-permute-start(f32[1,128,1280]{2,1,0:T(8,128)S(1)} %collective-permute-done.7), channel_id=1, source_target_pairs={{0,1},{1,0},{2,3},{3,2},{4,5},{5,4},{6,7},{7,6},{8,9},{9,8},{10,11... | collective-permute-start | bytes 1966088 | tf_op jit(solution)/shard_map/ppermute | solution.py:17
  55.6 3.0 %copy-start.2 = (f32[1,1,128,128]{3,2,0,1:T(8,128)}, f32[1,1,128,128]{3,2,0,1:T(8,128)S(1)}, u32[]{:S(2)}) copy-start(f32[1,1,128,128]{3,2,0,1:T(8,128)S(1)} %convolution_bitcast_fusion.8) | copy-start | bytes 196612
  55.6 28.8 %collective-permute-start.6 = (f32[1,1,128,128]{3,2,0,1:T(8,128)S(1)}, f32[1,1,128,128]{3,2,0,1:T(8,128)S(1)}, u32[]{:S(2)}, u32[]{:S(2)}) collective-permute-start(f32[1,1,128,128]{3,2,0,1:T(8,128)S(1)} %convolution_bitcast_fusion.8), channel_id=1, source_target_pairs={{0,1},{1,0},{2,3},{3,2},{4,5},{5,4},{6,7},{7,6},{8,9},{9,8},{10,11... | collective-permute-start | bytes 196616 | tf_op jit(solution)/shard_map/ppermute | solution.py:17
  84.4 0.6 copy-start.6
  85.0 1.0 copy-start.3
  87.6 26.5 %collective-permute-start.13 = (f32[1,128,1280]{2,1,0:T(8,128)}, f32[1,128,1280]{2,1,0:T(8,128)}, u32[]{:S(2)}, u32[]{:S(2)}) collective-permute-start(f32[1,128,1280]{2,1,0:T(8,128)} %convolution_bitcast_fusion.2), channel_id=1, source_target_pairs={{0,1},{1,0},{2,3},{3,2},{4,5},{5,4},{6,7},{7,6},{8,9},{9,8},{10,11... | collective-permute-start | bytes 1966088 | tf_op jit(solution)/shard_map/ppermute | solution.py:17
  91.7 17.7 %collective-permute-start.10 = (f32[1,1,128,128]{2,3,0,1:T(8,128)S(1)}, f32[1,1,128,128]{2,3,0,1:T(8,128)S(1)}, u32[]{:S(2)}, u32[]{:S(2)}) collective-permute-start(f32[1,1,128,128]{2,3,0,1:T(8,128)S(1)} %convolution_bitcast_fusion.6), channel_id=1, source_target_pairs={{0,1},{1,0},{2,3},{3,2},{4,5},{5,4},{6,7},{7,6},{8,9},{9,8},{10,11... | collective-permute-start | bytes 196616 | tf_op jit(solution)/shard_map/ppermute | solution.py:17
  99.4 10.0 %copy-start.8 = (f32[128]{0:T(128)S(1)}, f32[128]{0:T(128)}, u32[]{:S(2)}) copy-start(f32[128]{0:T(128)} %get-tuple-element.5) | copy-start | bytes 1540
  99.4 16.6 %collective-permute-start.12 = (f32[1,128,1280]{2,1,0:T(8,128)}, f32[1,128,1280]{2,1,0:T(8,128)}, u32[]{:S(2)}, u32[]{:S(2)}) collective-permute-start(f32[1,128,1280]{2,1,0:T(8,128)} %fusion.5), channel_id=1, source_target_pairs={{480,0},{0,32},{32,64},{64,96},{96,128},{128,160},{160,192},{192,2... | collective-permute-start | bytes 1966088 | tf_op jit(solution)/shard_map/ppermute | solution.py:13
  111.8 19.7 %collective-permute-start.15 = (f32[1,128,1280]{2,1,0:T(8,128)}, f32[1,128,1280]{2,1,0:T(8,128)}, u32[]{:S(2)}, u32[]{:S(2)}) collective-permute-start(f32[1,128,1280]{2,1,0:T(8,128)} %convolution_bitcast_fusion), channel_id=1, source_target_pairs={{0,1},{1,0},{2,3},{3,2},{4,5},{5,4},{6,7},{7,6},{8,9},{9,8},{10,11... | collective-permute-start | bytes 1966088 | tf_op jit(solution)/shard_map/ppermute | solution.py:17
  115.9 4.1 %copy-start.5 = (f32[1,1,128,128]{2,3,0,1:T(8,128)S(1)}, f32[1,1,128,128]{2,3,0,1:T(8,128)}, u32[]{:S(2)}) copy-start(f32[1,1,128,128]{2,3,0,1:T(8,128)} %copy.9) | copy-start | bytes 196612
  118.0 15.4 %collective-permute-start.14 = (f32[1,128,1280]{2,1,0:T(8,128)}, f32[1,128,1280]{2,1,0:T(8,128)}, u32[]{:S(2)}, u32[]{:S(2)}) collective-permute-start(f32[1,128,1280]{2,1,0:T(8,128)} %add.74), channel_id=1, source_target_pairs={{480,0},{0,32},{32,64},{64,96},{96,128},{128,160},{160,192},{192,2... | collective-permute-start | bytes 1966088 | tf_op jit(solution)/shard_map/ppermute | solution.py:13
  135.3 106.1 %collective-permute-start.16 = (f32[1,128,1280]{2,1,0:T(8,128)}, f32[1,128,1280]{2,1,0:T(8,128)}, u32[]{:S(2)}, u32[]{:S(2)}) collective-permute-start(f32[1,128,1280]{2,1,0:T(8,128)} %add.76), channel_id=1, source_target_pairs={{64,0},{96,32},{128,64},{160,96},{192,128},{224,160},{256,192},{28... | collective-permute-start | bytes 1966088 | tf_op jit(solution)/shard_map/ppermute | solution.py:13
where the time goes:
time: 245 us; the launch traced here: 244 us
  blocking collectives  95.2 us (39%)
  starting transfers between devices  54.4 us (22%)
  waiting for transfers between devices  49.6 us (20%)
  matrix products  27.3 us (11%)
  other arithmetic  8.96 us (4%)
  between operations  4.94 us (2%)
  local copies, waits for them, and re-layouts  3.79 us (2%)
    psum x1, blocking collectives, local(): pair_trace = lax.psum(jnp.concatenate(traces, axis=1), 'vir')  95.2 us
    ppermute x10, waiting for transfers between devices, partner(): lax.ppermute(value, axis, [(i, i ^ 1 << apart) for i in range(lax.axis_si...  47.2 us
    ppermute x10, starting transfers between devices, partner(): lax.ppermute(value, axis, [(i, i ^ 1 << apart) for i in range(lax.axis_si...  34 us
    dot_general x18, matrix products, contract(): jnp.einsum(pattern, former, latter, precision=lax.Precision.HIGHEST, pref...  27.3 us
    ppermute x7, starting transfers between devices, passed_along(): return lax.ppermute(block, axis, route)  20.5 us
  transfers between devices with their start and end apart: 17, of which 6 were waited for; matrix products, arithmetic and copies ran while one was open for 14% of the time, Pallas kernels for 0%

commit v1 on v0

v1 whole, which is shorter than its diff:
```python
import jax
import jax.numpy as jnp
from jax import lax
from jax.experimental import pallas as pl
from jax.experimental.pallas import tpu as pltpu
from jax.sharding import PartitionSpec as P

NVIR = 4096
NAUX = 1280
ROWS = 128
NCH = 4
CH = ROWS // NCH
COLS = 256
MESH = pl.DeviceIdType.MESH
F32 = jnp.float32
BF16 = jnp.bfloat16

OWN, SIB, UP, DOWN, REST = range(5)
(
    S_SIB, S_UP, S_DOWN, S_PART, S_REST, S_FAR_UP, S_FAR_DOWN, S_FAR_SIB, S_FAR_REST,
    S_WRAP, S_CROSS,
) = range(11)


def halves(value):
    high = value.astype(BF16)
    return high, (value - high.astype(F32)).astype(BF16)


def rows_dot(former, latter):
    dims = (((1,), (1,)), ((), ()))

    def dot(a, b):
        return lax.dot_general(a, b, dims, preferred_element_type=F32)

    return dot(former[0], latter[0]) + (dot(former[0], latter[1]) + dot(former[1], latter[0]))


def folded(tile):
    return jnp.sum(tile.reshape(tile.shape[0] // 8, 8, 128), axis=0)


def kernel(
    factor, occ, vir, density, trace,
    own, near, far, staged, near_h, near_l, far_h, far_l, crossed, energy, energies, sums,
    tile_out, tile_in, next_out, next_in,
    own_sem, send_sem, near_sem, far_sem, staged_sem, e_send, e_recv, t_send, t_recv,
):
    o = lax.axis_index("occ")
    v = lax.axis_index("vir")
    q = lax.rem(o, 2)
    x = lax.rem(o // 2, 4)
    y_lo = o // 8
    other_row = o + 8 - 16 * y_lo
    sibling = o + 1 - 2 * q
    mate = v + 1 - 2 * lax.rem(v, 2)
    first = x == 0
    last = x == 3
    edge = jnp.logical_or(first, last)
    inner = jnp.logical_not(edge)
    across = jnp.where(last, o - 6, o + 6)

    def occ_at(distance):
        return lax.rem(o + distance + 16, 16)

    up, down = occ_at(2), occ_at(-2)
    beyond = jnp.where(last, up, down)

    def flipped(r):
        z = v
        out = v
        for bit in (1, 2, 4, 8, 16):
            if r & bit:
                out = out + bit - 2 * bit * lax.rem(z // bit, 2)
        return out

    own_copy = pltpu.make_async_copy(factor.at[0], own, own_sem)
    own_copy.start()

    barrier = pltpu.get_barrier_semaphore()
    peers = [(occ_at(d), v) for d in (1, -1, 2, -2)]
    peers += [(o, flipped(r)) for r in (1, 2, 3, 4, 5, 6, 7, 8, 16, 24)]
    for peer in peers:
        pl.semaphore_signal(barrier, inc=1, device_id=peer, device_id_type=MESH)

    @pl.when(edge)
    def _():
        for peer in ((other_row, v), (across, v), (other_row, mate), (beyond, mate)):
            pl.semaphore_signal(barrier, inc=1, device_id=peer, device_id_type=MESH)

    energy[...] = jnp.zeros((8, 128), F32)
    energy[0:1, :] = vir[...]
    energy[1:2, :] = jnp.broadcast_to(occ[...], (1, 128))

    pl.semaphore_wait(barrier, jnp.where(edge, len(peers) + 4, len(peers)))

    def remote(src, dst, send, recv, device):
        return pltpu.make_async_remote_copy(
            src_ref=src, dst_ref=dst, send_sem=send, recv_sem=recv,
            device_id=device, device_id_type=MESH,
        )

    def part(ref, n):
        return ref.at[pl.ds(n * CH, CH)]

    def mine(n):
        return factor.at[0, pl.ds(n * CH, CH)]

    def to_near(src, slot, n, flow, device):
        return remote(
            src, near.at[slot, pl.ds(n * CH, CH)], send_sem.at[flow, n], near_sem.at[slot, n], device
        )

    def to_far(src, slot, n, flow, device):
        return remote(
            src, far.at[slot, pl.ds(n * CH, CH)], send_sem.at[flow, n], far_sem.at[slot, n], device
        )

    def to_staged(n):
        return remote(
            mine(n), part(staged, n), send_sem.at[S_PART, n], staged_sem.at[n], (other_row, v)
        )

    def near_part(slot, n):
        return near.at[slot, pl.ds(n * CH, CH)]

    def far_part(slot, n):
        return far.at[slot, pl.ds(n * CH, CH)]

    def sib_side(slot, n):
        return slot

    e_peers = [(occ_at(1), v), (occ_at(-1), v), (occ_at(2), v), (occ_at(-2), v), (o, mate)]
    e_copies = [
        remote(energy, energies.at[k], e_send.at[k], e_recv.at[k], peer)
        for k, peer in enumerate(e_peers)
    ]
    for copy in e_copies:
        copy.start()

    for n in range(NCH):
        @pl.when(edge)
        def _():
            to_staged(n).start()

        @pl.when(inner)
        def _():
            to_far(mine(n), 0, n, S_PART, (o, mate)).start()

        @pl.when(jnp.logical_not(last))
        def _():
            to_near(mine(n), DOWN, n, S_UP, (up, v)).start()

        @pl.when(jnp.logical_not(first))
        def _():
            to_near(mine(n), UP, n, S_DOWN, (down, v)).start()

        to_near(mine(n), SIB, n, S_SIB, (sibling, v)).start()

    def wait_near(slot, n):
        to_near(near_part(slot, n), slot, n, S_SIB, (sibling, v)).wait_recv()

    def wait_far(slot, n):
        to_far(far_part(slot, n), slot, n, S_SIB, (sibling, v)).wait_recv()

    def relay_staged(n):
        @pl.when(edge)
        def _():
            to_staged(n).wait_recv()
            to_near(part(staged, n), jnp.where(last, DOWN, UP), n, S_WRAP, (across, v)).start()
            to_far(part(staged, n), 0, n, S_CROSS, (other_row, mate)).start()

    def relay_partner(n):
        wait_far(0, n)

        @pl.when(jnp.logical_not(last))
        def _():
            to_far(far_part(0, n), DOWN, n, S_FAR_UP, (up, v)).start()

        @pl.when(last)
        def _():
            to_far(mine(n), DOWN, n, S_FAR_UP, (up, mate)).start()

        @pl.when(jnp.logical_not(first))
        def _():
            to_far(far_part(0, n), UP, n, S_FAR_DOWN, (down, v)).start()

        @pl.when(first)
        def _():
            to_far(mine(n), UP, n, S_FAR_DOWN, (down, mate)).start()

        to_far(far_part(0, n), SIB, n, S_FAR_SIB, (sibling, v)).start()

    passed = jnp.where(q == 0, UP, DOWN)

    def relay_near(n):
        wait_near(UP, n)
        wait_near(DOWN, n)
        to_near(near_part(passed, n), REST, n, S_REST, (sibling, v)).start()

    def relay_far(n):
        wait_far(UP, n)
        wait_far(DOWN, n)
        to_far(far_part(passed, n), REST, n, S_FAR_REST, (sibling, v)).start()

    def split_near(slot, start, count):
        rows = pl.ds(slot * ROWS + start, count)
        h, l = halves(near[slot, pl.ds(start, count), :])
        near_h[rows, :] = h
        near_l[rows, :] = l

    def split_far(slot, start, count):
        rows = pl.ds(slot * ROWS + start, count)
        h, l = halves(far[slot, pl.ds(start, count), :])
        far_h[rows, :] = h
        far_l[rows, :] = l

    def near_rows(slot, count=1):
        rows = pl.ds(slot * ROWS, count * ROWS)
        return near_h[rows, :], near_l[rows, :]

    def add_density(weights, latter_h, latter_l, fresh=False):
        w_h, w_l = halves(weights)
        for c in range(NAUX // COLS):
            cols = pl.ds(c * COLS, COLS)
            h, l = latter_h[:, cols], latter_l[:, cols]
            term = (
                jnp.dot(w_h, h, preferred_element_type=F32)
                + jnp.dot(w_h, l, preferred_element_type=F32)
                + jnp.dot(w_l, h, preferred_element_type=F32)
            )
            density[0, :, cols] = term if fresh else density[0, :, cols] + term

    def pair_energy(slot):
        if slot == OWN:
            row = energy[1:2, :]
        elif slot == UP:
            row = energies[3, 1:2, :]
        elif slot == DOWN:
            row = energies[2, 1:2, :]
        elif slot == SIB:
            row = jnp.where(q == 0, energies[1, 1:2, :], energies[0, 1:2, :])
        else:
            row = jnp.where(q == 0, energies[0, 1:2, :], energies[1, 1:2, :])
        return row + energy[1:2, :]

    def diag_weights(k_tile, slot):
        across_b = jnp.broadcast_to(energy[0:1, :], (ROWS, 128))
        gap = pair_energy(slot) - across_b.T - across_b
        amp = k_tile / gap
        bar = 2.0 * amp - amp.T
        sums[slot] = folded(amp * bar)
        return 2.0 * bar if slot == OWN else bar

    relay_staged(0)
    own_copy.wait()
    h, l = halves(own[...])
    near_h[0:ROWS, :] = h
    near_l[0:ROWS, :] = l
    for copy in e_copies:
        copy.wait()
    for n in range(NCH):
        wait_near(SIB, n)
    split_near(SIB, 0, ROWS)
    k_first = rows_dot(near_rows(OWN), near_rows(OWN, 2))
    bars = jnp.concatenate(
        [diag_weights(k_first[:, :128], OWN), diag_weights(k_first[:, 128:], SIB)], axis=1
    )
    add_density(bars, near_h.at[0:256], near_l.at[0:256], fresh=True)

    for n in range(1, NCH + 1):
        if n < NCH:
            relay_staged(n)
        relay_partner(n - 1)
        relay_near(n - 1)
        start = (n - 1) * CH
        split_far(0, start, CH)
        split_near(UP, start, CH)
        split_near(DOWN, start, CH)

    k_next = rows_dot(near_rows(OWN), near_rows(UP, 2))
    bars = jnp.concatenate(
        [diag_weights(k_next[:, :128], UP), diag_weights(k_next[:, 128:], DOWN)], axis=1
    )
    add_density(bars, near_h.at[256:512], near_l.at[256:512])
    for n in range(NCH):
        wait_near(REST, n)
    split_near(REST, 0, ROWS)
    k_rest = rows_dot(near_rows(OWN), near_rows(REST))
    add_density(diag_weights(k_rest, REST), near_h.at[512:640], near_l.at[512:640])

    far_row = jnp.broadcast_to(energies[4, 0:1, :], (ROWS, 128)).T
    own_row = jnp.broadcast_to(energy[0:1, :], (ROWS, 128))
    partner = (far_h[0:ROWS, :], far_l[0:ROWS, :])
    for slot in range(5):
        k_tile = rows_dot(partner, near_rows(slot))
        crossed[slot] = k_tile / (pair_energy(slot) - far_row - own_row)
    weights = crossed[OWN]
    sums[OWN] += folded(weights * weights)
    add_density(2.0 * weights.T, far_h.at[0:ROWS], far_l.at[0:ROWS])

    mix_h, mix_l = tile_h, tile_l = None, None
    own_pair = near_rows(OWN)
    for n in range(NCH):
        relay_far(n)
        start = n * CH
        wait_far(SIB, n)
        wait_far(REST, n)
        pieces = [halves(far[slot, pl.ds(start, CH), :]) for slot in (SIB, UP, DOWN, REST)]
        lot_h = jnp.concatenate([p[0] for p in pieces], axis=0)
        lot_l = jnp.concatenate([p[1] for p in pieces], axis=0)
        far_h[0:4 * CH, :] = lot_h
        far_l[0:4 * CH, :] = lot_l
        k_tile = rows_dot((far_h[0:4 * CH, :], far_l[0:4 * CH, :]), own_pair)
        bars = []
        side = far_row[start:start + CH, :]
        for at, slot in enumerate((SIB, UP, DOWN, REST)):
            gap = pair_energy(slot) - side - own_row[0:CH, :]
            amp = k_tile[at * CH:(at + 1) * CH, :] / gap
            bar = 2.0 * amp - crossed[slot, pl.ds(start, CH), :]
            sums[slot] += folded(amp * bar)
            bars.append(bar)
        weights = jnp.concatenate(bars, axis=0).T
        if n == NCH - 1:
            before = jnp.where(q == 0, sums[REST], sums[SIB])
            tile_out[...] = jnp.zeros((8, 128), F32)
            tile_out[0:1, :] = jnp.sum(sums[OWN], axis=0, keepdims=True)
            tile_out[1:2, :] = jnp.sum(before, axis=0, keepdims=True)
            tile_out[2:3, :] = jnp.sum(sums[DOWN], axis=0, keepdims=True)
            round_one = [
                remote(tile_out, tile_in.at[r - 1], t_send.at[r - 1], t_recv.at[r - 1], (o, flipped(r)))
                for r in range(1, 8)
            ]
            for copy in round_one:
                copy.start()
        add_density(weights, far_h.at[0:4 * CH], far_l.at[0:4 * CH])

    total = tile_out[...]
    for copy in round_one:
        copy.wait_recv()
    for r in range(7):
        total = total + tile_in[r]
    next_out[...] = total
    round_two = [
        remote(next_out, next_in.at[k], t_send.at[7 + k], t_recv.at[7 + k], (o, flipped(r)))
        for k, r in enumerate((8, 16, 24))
    ]
    for copy in round_two:
        copy.start()
    for copy in round_one:
        copy.wait_send()

    for n in range(NCH):
        for flow in (S_SIB, S_PART, S_REST, S_FAR_UP, S_FAR_DOWN, S_FAR_SIB, S_FAR_REST):
            to_near(near_part(SIB, n), SIB, n, flow, (sibling, v)).wait_send()

        @pl.when(jnp.logical_not(last))
        def _():
            to_near(near_part(SIB, n), SIB, n, S_UP, (sibling, v)).wait_send()

        @pl.when(jnp.logical_not(first))
        def _():
            to_near(near_part(SIB, n), SIB, n, S_DOWN, (sibling, v)).wait_send()

        @pl.when(edge)
        def _():
            to_near(near_part(SIB, n), SIB, n, S_WRAP, (sibling, v)).wait_send()
            to_near(near_part(SIB, n), SIB, n, S_CROSS, (sibling, v)).wait_send()

    for copy in round_two:
        copy.wait()
    for k in range(3):
        total = total + next_in[k]
    summed = jnp.sum(total, axis=1, keepdims=True) / NVIR
    for k in range(3):
        trace[0:1, k:k + 1] = summed[k:k + 1, :]


def local(factor, occ_energy, vir_energy):
    vmem = pl.BlockSpec(memory_space=pltpu.VMEM)
    dma = pltpu.SemaphoreType.DMA
    block = (ROWS, NAUX)
    return pl.pallas_call(
        kernel,
        out_shape=(
            jax.ShapeDtypeStruct((1,) + block, F32),
            jax.ShapeDtypeStruct((1, 3), F32),
        ),
        in_specs=[pl.BlockSpec(memory_space=pltpu.HBM), vmem, vmem],
        out_specs=(vmem, vmem),
        scratch_shapes=[
            pltpu.VMEM(block, F32),
            pltpu.VMEM((5,) + block, F32),
            pltpu.VMEM((5,) + block, F32),
            pltpu.VMEM(block, F32),
            pltpu.VMEM((5 * ROWS, NAUX), BF16),
            pltpu.VMEM((5 * ROWS, NAUX), BF16),
            pltpu.VMEM(block, BF16),
            pltpu.VMEM(block, BF16),
            pltpu.VMEM((5, ROWS, 128), F32),
            pltpu.VMEM((8, 128), F32),
            pltpu.VMEM((5, 8, 128), F32),
            pltpu.VMEM((5, 8, 128), F32),
            pltpu.VMEM((8, 128), F32),
            pltpu.VMEM((7, 8, 128), F32),
            pltpu.VMEM((8, 128), F32),
            pltpu.VMEM((3, 8, 128), F32),
            dma,
            dma((11, NCH)),
            dma((5, NCH)),
            dma((5, NCH)),
            dma((NCH,)),
            dma((5,)),
            dma((5,)),
            dma((10,)),
            dma((10,)),
        ],
        compiler_params=pltpu.CompilerParams(
            collective_id=0, has_side_effects=True, vmem_limit_bytes=48 << 20
        ),
        cost_estimate=pl.CostEstimate(
            flops=6 * 24 * ROWS * ROWS * NAUX, bytes_accessed=2 * 4 * ROWS * NAUX, transcendentals=0
        ),
    )(factor, occ_energy.reshape(1, 1), vir_energy.reshape(1, 128))


def solution(mesh):
    placed = (P("occ", "vir", None), P("occ"), P("vir"))
    return jax.shard_map(
        local,
        mesh=mesh,
        in_specs=placed,
        out_specs=(P("occ", "vir", None), P("occ", None)),
        check_vma=False,
    )
```

time: 245 us -> 75.5 us (0.31)
  the two profiles are of different devices: /device:TPU:2 before, /device:TPU:1 now
where the time goes in v1:
time: 75.5 us; the launch traced here: 75.2 us
  Pallas kernels  70.8 us (94%)
  local copies, waits for them, and re-layouts  3.08 us (4%)
  between operations  1.29 us (2%)
    pallas_call x1, Pallas kernels, local(): pl.pallas_call(kernel, out_shape=(jax.ShapeDtypeStruct((1,) + block, F32)...  70.8 us
    unnamed x6, local copies, waits for them, and re-layouts  3.08 us

profile of v1, /device:TPU:1, one launch (start us, length us, event | category | flops | bytes accessed | tf_op | source)
XLA Modules:
  0.0 75.2 jit_solution(8249808006510710316)
XLA Ops:
  1.3 0.0 copy-start.1
  1.3 0.6 copy-done.1
  1.9 0.0 copy-start
  1.9 1.1 %copy-done = f32[1,128,1280]{2,1,0:T(8,128)S(1)} copy-done((f32[1,128,1280]{2,1,0:T(8,128)S(1)}, f32[1,128,1280]{2,1,0:T(8,128)}, u32[]{:S(2)}) %copy-start) | copy-done | bytes 655384
  3.0 70.8 %shard_map.50 = (f32[1,128,1280]{2,1,0:T(8,128)S(1)}, f32[1,3]{1,0:T(1,128)S(1)}) custom-call(f32[1,128,1280]{2,1,0:T(8,128)S(1)} %copy-done, f32[1,1]{1,0:T(1,128)} %bitcast.2.occ, f32[1,128]{1,0:T(1,128)S(1)} %bitcast.3), custom_call_target="tpu_custom_call" | custom-call | flops 3019898880 | bytes 1310720 | tf_op jit(solution)/shard_map/pallas_call | solution.py:383
  73.9 0.8 %copy.8 = f32[1,128,1280]{2,1,0:T(8,128)} copy(f32[1,128,1280]{2,1,0:T(8,128)S(1)} %get-tuple-element.4) | data formatting | bytes 1310720
  74.7 0.5 copy.9
Async XLA Ops:
  1.3 0.7 copy-start.1
  1.9 1.1 %copy-start = (f32[1,128,1280]{2,1,0:T(8,128)S(1)}, f32[1,128,1280]{2,1,0:T(8,128)}, u32[]{:S(2)}) copy-start(f32[1,128,1280]{2,1,0:T(8,128)} %factor.1) | copy-start | bytes 1966084

commit v2 on v1

--- a/solution.py
+++ b/solution.py
@@ -43,8 +43,9 @@
 def kernel(
     factor, occ, vir, density, trace,
     own, near, far, staged, near_h, near_l, far_h, far_l, crossed, energy, energies, sums,
-    tile_out, tile_in, next_out, next_in,
+    other_tile, tile_out, tile_in, next_out, next_in,
     own_sem, send_sem, near_sem, far_sem, staged_sem, e_send, e_recv, t_send, t_recv,
+    x_send, x_recv, entered,
 ):
     o = lax.axis_index("occ")
     v = lax.axis_index("vir")
@@ -66,20 +67,17 @@
     up, down = occ_at(2), occ_at(-2)
     beyond = jnp.where(last, up, down)
 
-    def flipped(r):
-        z = v
-        out = v
-        for bit in (1, 2, 4, 8, 16):
-            if r & bit:
-                out = out + bit - 2 * bit * lax.rem(z // bit, 2)
-        return out
+    half = lax.rem(v, 2)
+
+    def vir_at(distance):
+        return lax.rem(v + 2 * distance + 32, 32)
 
     own_copy = pltpu.make_async_copy(factor.at[0], own, own_sem)
     own_copy.start()
 
     barrier = pltpu.get_barrier_semaphore()
     peers = [(occ_at(d), v) for d in (1, -1, 2, -2)]
-    peers += [(o, flipped(r)) for r in (1, 2, 3, 4, 5, 6, 7, 8, 16, 24)]
+    peers += [(o, mate), (o, vir_at(1)), (o, vir_at(-1))]
     for peer in peers:
         pl.semaphore_signal(barrier, inc=1, device_id=peer, device_id_type=MESH)
 
@@ -126,9 +124,6 @@
 
     def far_part(slot, n):
         return far.at[slot, pl.ds(n * CH, CH)]
-
-    def sib_side(slot, n):
-        return slot
 
     e_peers = [(occ_at(1), v), (occ_at(-1), v), (occ_at(2), v), (occ_at(-2), v), (o, mate)]
     e_copies = [
@@ -138,10 +133,22 @@
     for copy in e_copies:
         copy.start()
 
+    def far_wrap(n):
+        @pl.when(last)
+        def _():
+            to_far(mine(n), DOWN, n, S_FAR_UP, (up, mate)).start()
+
+        @pl.when(first)
+        def _():
+            to_far(mine(n), UP, n, S_FAR_DOWN, (down, mate)).start()
+
     for n in range(NCH):
         @pl.when(edge)
         def _():
             to_staged(n).start()
+
+        if n == 0:
+            far_wrap(0)
 
         @pl.when(inner)
         def _():
@@ -177,18 +184,12 @@
         def _():
             to_far(far_part(0, n), DOWN, n, S_FAR_UP, (up, v)).start()
 
-        @pl.when(last)
-        def _():
-            to_far(mine(n), DOWN, n, S_FAR_UP, (up, mate)).start()
-
         @pl.when(jnp.logical_not(first))
         def _():
             to_far(far_part(0, n), UP, n, S_FAR_DOWN, (down, v)).start()
 
-        @pl.when(first)
-        def _():
-            to_far(mine(n), UP, n, S_FAR_DOWN, (down, mate)).start()
-
+        if n + 1 < NCH:
+            far_wrap(n + 1)
         to_far(far_part(0, n), SIB, n, S_FAR_SIB, (sibling, v)).start()
 
     passed = jnp.where(q == 0, UP, DOWN)
@@ -252,6 +253,19 @@
         sums[slot] = folded(amp * bar)
         return 2.0 * bar if slot == OWN else bar
 
+    def greet(step):
+        pl.semaphore_signal(
+            entered.at[step, 0], inc=1, device_id=(o, vir_at(-(1 << step))), device_id_type=MESH
+        )
+        pl.semaphore_signal(
+            entered.at[step, 1], inc=1, device_id=(o, vir_at(1 << step)), device_id_type=MESH
+        )
+
+    def greeted(step):
+        pl.semaphore_wait(entered.at[step, 0], 1)
+        pl.semaphore_wait(entered.at[step, 1], 1)
+
+    greet(0)
     relay_staged(0)
     own_copy.wait()
     h, l = halves(own[...])
@@ -273,80 +287,103 @@
             relay_staged(n)
         relay_partner(n - 1)
         relay_near(n - 1)
+        if n <= 3:
+            greeted(n - 1)
+            if n < 3:
+                greet(n)
         start = (n - 1) * CH
         split_far(0, start, CH)
         split_near(UP, start, CH)
         split_near(DOWN, start, CH)
 
-    k_next = rows_dot(near_rows(OWN), near_rows(UP, 2))
-    bars = jnp.concatenate(
-        [diag_weights(k_next[:, :128], UP), diag_weights(k_next[:, 128:], DOWN)], axis=1
-    )
-    add_density(bars, near_h.at[256:512], near_l.at[256:512])
     for n in range(NCH):
         wait_near(REST, n)
     split_near(REST, 0, ROWS)
-    k_rest = rows_dot(near_rows(OWN), near_rows(REST))
-    add_density(diag_weights(k_rest, REST), near_h.at[512:640], near_l.at[512:640])
 
     far_row = jnp.broadcast_to(energies[4, 0:1, :], (ROWS, 128)).T
     own_row = jnp.broadcast_to(energy[0:1, :], (ROWS, 128))
     partner = (far_h[0:ROWS, :], far_l[0:ROWS, :])
+    k_cross = rows_dot(partner, near_rows(OWN, 5))
     for slot in range(5):
-        k_tile = rows_dot(partner, near_rows(slot))
-        crossed[slot] = k_tile / (pair_energy(slot) - far_row - own_row)
-    weights = crossed[OWN]
-    sums[OWN] += folded(weights * weights)
-    add_density(2.0 * weights.T, far_h.at[0:ROWS], far_l.at[0:ROWS])
-
-    mix_h, mix_l = tile_h, tile_l = None, None
+        amp = k_cross[:, slot * 128:(slot + 1) * 128] / (pair_energy(slot) - far_row - own_row)
+        crossed[slot] = amp
+        squares = folded(amp * amp)
+        sums[5 + slot] = squares if slot == OWN else 2.0 * squares
+
+    swap = remote(
+        crossed.at[jnp.where(half == 0, jnp.where(q == 0, SIB, REST), UP)],
+        other_tile, x_send, x_recv, (jnp.where(half == 0, occ_at(1), up), v),
+    )
+    swap.start()
+
+    k_next = rows_dot(near_rows(OWN), near_rows(UP, 3))
+    bars = jnp.concatenate(
+        [diag_weights(k_next[:, at * 128:(at + 1) * 128], slot) for at, slot in enumerate((UP, DOWN, REST))],
+        axis=1,
+    )
+    add_density(bars, near_h.at[256:640], near_l.at[256:640])
+    add_density(2.0 * crossed[OWN].T, far_h.at[0:ROWS], far_l.at[0:ROWS])
+
+    def trace_one():
+        swap.wait()
+        here = crossed[jnp.where(half == 0, jnp.where(q == 0, REST, SIB), DOWN)]
+        product = 2.0 * folded(here * other_tile[...])
+        before = jnp.where(q == 0, sums[REST] + sums[5 + REST], sums[SIB] + sums[5 + SIB])
+        before = before - jnp.where(half == 0, product, 0.0)
+        second = sums[DOWN] + sums[5 + DOWN] - jnp.where(half == 0, 0.0, product)
+        tile_out[...] = jnp.zeros((8, 128), F32)
+        tile_out[0:1, :] = jnp.sum(sums[OWN] + sums[5 + OWN], axis=0, keepdims=True)
+        tile_out[1:2, :] = jnp.sum(before, axis=0, keepdims=True)
+        tile_out[2:3, :] = jnp.sum(second, axis=0, keepdims=True)
+        for copy in round_one:
+            copy.start()
+
+    def trace_two():
+        total = tile_out[...]
+        for copy in round_one:
+            copy.wait_recv()
+        for r in range(7):
+            total = total + tile_in[r]
+        next_out[...] = total
+        for copy in round_two:
+            copy.start()
+
+    near_z = [(0, mate)] + [(d, side) for d in (1, 2, 3) for side in (v, mate)]
+    round_one = [
+        remote(
+            tile_out, tile_in.at[k], t_send.at[k], t_recv.at[k],
+            (o, lax.rem(side + 2 * d, 32)),
+        )
+        for k, (d, side) in enumerate(near_z)
+    ]
+    round_two = [
+        remote(next_out, next_in.at[k], t_send.at[7 + k], t_recv.at[7 + k], (o, vir_at(d)))
+        for k, d in enumerate((4, 8, -4))
+    ]
+
     own_pair = near_rows(OWN)
     for n in range(NCH):
         relay_far(n)
         start = n * CH
         wait_far(SIB, n)
         wait_far(REST, n)
-        pieces = [halves(far[slot, pl.ds(start, CH), :]) for slot in (SIB, UP, DOWN, REST)]
-        lot_h = jnp.concatenate([p[0] for p in pieces], axis=0)
-        lot_l = jnp.concatenate([p[1] for p in pieces], axis=0)
-        far_h[0:4 * CH, :] = lot_h
-        far_l[0:4 * CH, :] = lot_l
-        k_tile = rows_dot((far_h[0:4 * CH, :], far_l[0:4 * CH, :]), own_pair)
+        for at, slot in enumerate((SIB, UP, DOWN, REST)):
+            h, l = halves(far[slot, pl.ds(start, CH), :])
+            far_h[at * CH:(at + 1) * CH, :] = h
+            far_l[at * CH:(at + 1) * CH, :] = l
+        k_tile = rows_dot((far_h[...], far_l[...]), own_pair)
         bars = []
         side = far_row[start:start + CH, :]
         for at, slot in enumerate((SIB, UP, DOWN, REST)):
             gap = pair_energy(slot) - side - own_row[0:CH, :]
             amp = k_tile[at * CH:(at + 1) * CH, :] / gap
-            bar = 2.0 * amp - crossed[slot, pl.ds(start, CH), :]
-            sums[slot] += folded(amp * bar)
-            bars.append(bar)
-        weights = jnp.concatenate(bars, axis=0).T
-        if n == NCH - 1:
-            before = jnp.where(q == 0, sums[REST], sums[SIB])
-            tile_out[...] = jnp.zeros((8, 128), F32)
-            tile_out[0:1, :] = jnp.sum(sums[OWN], axis=0, keepdims=True)
-            tile_out[1:2, :] = jnp.sum(before, axis=0, keepdims=True)
-            tile_out[2:3, :] = jnp.sum(sums[DOWN], axis=0, keepdims=True)
-            round_one = [
-                remote(tile_out, tile_in.at[r - 1], t_send.at[r - 1], t_recv.at[r - 1], (o, flipped(r)))
-                for r in range(1, 8)
-            ]
-            for copy in round_one:
-                copy.start()
-        add_density(weights, far_h.at[0:4 * CH], far_l.at[0:4 * CH])
-
-    total = tile_out[...]
-    for copy in round_one:
-        copy.wait_recv()
-    for r in range(7):
-        total = total + tile_in[r]
-    next_out[...] = total
-    round_two = [
-        remote(next_out, next_in.at[k], t_send.at[7 + k], t_recv.at[7 + k], (o, flipped(r)))
-        for k, r in enumerate((8, 16, 24))
-    ]
-    for copy in round_two:
-        copy.start()
+            bars.append(2.0 * amp - crossed[slot, pl.ds(start, CH), :])
+        add_density(jnp.concatenate(bars, axis=0).T, far_h, far_l)
+        if n == 0:
+            trace_one()
+        elif n == NCH - 2:
+            trace_two()
+
     for copy in round_one:
         copy.wait_send()
 
@@ -369,6 +406,7 @@
 
     for copy in round_two:
         copy.wait()
+    total = next_out[...]
     for k in range(3):
         total = total + next_in[k]
     summed = jnp.sum(total, axis=1, keepdims=True) / NVIR
@@ -400,7 +438,8 @@
             pltpu.VMEM((5, ROWS, 128), F32),
             pltpu.VMEM((8, 128), F32),
             pltpu.VMEM((5, 8, 128), F32),
-            pltpu.VMEM((5, 8, 128), F32),
+            pltpu.VMEM((10, 8, 128), F32),
+            pltpu.VMEM((ROWS, 128), F32),
             pltpu.VMEM((8, 128), F32),
             pltpu.VMEM((7, 8, 128), F32),
             pltpu.VMEM((8, 128), F32),
@@ -414,9 +453,12 @@
             dma((5,)),
             dma((10,)),
             dma((10,)),
+            dma,
+            dma,
+            pltpu.SemaphoreType.REGULAR((3, 2)),
         ],
         compiler_params=pltpu.CompilerParams(
-            collective_id=0, has_side_effects=True, vmem_limit_bytes=48 << 20
+            collective_id=0, has_side_effects=True, vmem_limit_bytes=62 << 20
         ),
         cost_estimate=pl.CostEstimate(
             flops=6 * 24 * ROWS * ROWS * NAUX, bytes_accessed=2 * 4 * ROWS * NAUX, transcendentals=0

time: 75.5 us -> 70.3 us (0.931)
  Pallas kernels: 70.8 us -> 66.3 us
    pallas_call x1, Pallas kernels: 70.8 us -> 66.3 us  [local(): pl.pallas_call(kernel, out_shape=(jax.ShapeDtypeStruct((1,) + block, F32)...]
    unnamed x6 -> x4, local copies, waits for them, and re-layouts: 3.08 us -> 2.48 us
where the time goes in v2:
time: 70.3 us; the launch traced here: 70.1 us
  Pallas kernels  66.3 us (94%)
  local copies, waits for them, and re-layouts  2.48 us (4%)
  between operations  1.29 us (2%)
    pallas_call x1, Pallas kernels, local(): pl.pallas_call(kernel, out_shape=(jax.ShapeDtypeStruct((1,) + block, F32)...  66.3 us
    unnamed x4, local copies, waits for them, and re-layouts  2.48 us

profile of v2, /device:TPU:1, one launch (start us, length us, event | category | flops | bytes accessed | tf_op | source)
XLA Modules:
  0.0 70.1 jit_solution(15745321938598737710)
XLA Ops:
  1.3 66.3 %shard_map.50 = (f32[1,128,1280]{2,1,0:T(8,128)}, f32[1,3]{1,0:T(1,128)}) custom-call(f32[1,128,1280]{2,1,0:T(8,128)} %factor.1, f32[1,1]{1,0:T(1,128)} %bitcast.2.occ, f32[1,128]{1,0:T(1,128)} %bitcast.3), custom_call_target="tpu_custom_call" | custom-call | flops 3019898880 | bytes 1310720 | tf_op jit(solution)/shard_map/pallas_call | solution.py:421
  67.6 0.0 copy-start
  67.6 2.0 %copy.8 = f32[1,128,1280]{2,1,0:T(8,128)} copy(f32[1,128,1280]{2,1,0:T(8,128)} %get-tuple-element.4) | data formatting | bytes 1310720
  69.6 0.0 copy-done
  69.6 0.5 copy.9
Async XLA Ops:
  67.6 2.0 %copy-start = (f32[1,3]{1,0:T(1,128)S(1)}, f32[1,3]{1,0:T(1,128)}, u32[]{:S(2)}) copy-start(f32[1,3]{1,0:T(1,128)} %get-tuple-element.5) | copy-start | bytes 40

commit v3 on v2

--- a/solution.py
+++ b/solution.py
@@ -68,16 +68,22 @@
     beyond = jnp.where(last, up, down)
 
     half = lax.rem(v, 2)
-
-    def vir_at(distance):
-        return lax.rem(v + 2 * distance + 32, 32)
+    z = v // 2
+    below, above = z > 0, z < 15
+
+    def flipped(r):
+        out = v
+        for bit in (1, 2, 4, 8, 16):
+            if r & bit:
+                out = out + bit - 2 * bit * lax.rem(v // bit, 2)
+        return out
 
     own_copy = pltpu.make_async_copy(factor.at[0], own, own_sem)
     own_copy.start()
 
     barrier = pltpu.get_barrier_semaphore()
     peers = [(occ_at(d), v) for d in (1, -1, 2, -2)]
-    peers += [(o, mate), (o, vir_at(1)), (o, vir_at(-1))]
+    peers += [(o, mate)]
     for peer in peers:
         pl.semaphore_signal(barrier, inc=1, device_id=peer, device_id_type=MESH)
 
@@ -86,11 +92,20 @@
         for peer in ((other_row, v), (across, v), (other_row, mate), (beyond, mate)):
             pl.semaphore_signal(barrier, inc=1, device_id=peer, device_id_type=MESH)
 
+    @pl.when(below)
+    def _():
+        pl.semaphore_signal(barrier, inc=1, device_id=(o, v - 2), device_id_type=MESH)
+
+    @pl.when(above)
+    def _():
+        pl.semaphore_signal(barrier, inc=1, device_id=(o, v + 2), device_id_type=MESH)
+
     energy[...] = jnp.zeros((8, 128), F32)
     energy[0:1, :] = vir[...]
     energy[1:2, :] = jnp.broadcast_to(occ[...], (1, 128))
 
-    pl.semaphore_wait(barrier, jnp.where(edge, len(peers) + 4, len(peers)))
+    at_end = jnp.where(jnp.logical_and(below, above), 0, 1)
+    pl.semaphore_wait(barrier, jnp.where(edge, len(peers) + 6, len(peers) + 2) - at_end)
 
     def remote(src, dst, send, recv, device):
         return pltpu.make_async_remote_copy(
@@ -177,9 +192,11 @@
             to_near(part(staged, n), jnp.where(last, DOWN, UP), n, S_WRAP, (across, v)).start()
             to_far(part(staged, n), 0, n, S_CROSS, (other_row, mate)).start()
 
+    def take_partner(n):
+        wait_far(0, n)
+        to_far(far_part(0, n), SIB, n, S_FAR_SIB, (sibling, v)).start()
+
     def relay_partner(n):
-        wait_far(0, n)
-
         @pl.when(jnp.logical_not(last))
         def _():
             to_far(far_part(0, n), DOWN, n, S_FAR_UP, (up, v)).start()
@@ -187,10 +204,6 @@
         @pl.when(jnp.logical_not(first))
         def _():
             to_far(far_part(0, n), UP, n, S_FAR_DOWN, (down, v)).start()
-
-        if n + 1 < NCH:
-            far_wrap(n + 1)
-        to_far(far_part(0, n), SIB, n, S_FAR_SIB, (sibling, v)).start()
 
     passed = jnp.where(q == 0, UP, DOWN)
 
@@ -254,16 +267,26 @@
         return 2.0 * bar if slot == OWN else bar
 
     def greet(step):
-        pl.semaphore_signal(
-            entered.at[step, 0], inc=1, device_id=(o, vir_at(-(1 << step))), device_id_type=MESH
-        )
-        pl.semaphore_signal(
-            entered.at[step, 1], inc=1, device_id=(o, vir_at(1 << step)), device_id_type=MESH
-        )
+        @pl.when(z >= 1 << step)
+        def _():
+            pl.semaphore_signal(
+                entered.at[step, 0], inc=1, device_id=(o, v - (2 << step)), device_id_type=MESH
+            )
+
+        @pl.when(z < 16 - (1 << step))
+        def _():
+            pl.semaphore_signal(
+                entered.at[step, 1], inc=1, device_id=(o, v + (2 << step)), device_id_type=MESH
+            )
 
     def greeted(step):
-        pl.semaphore_wait(entered.at[step, 0], 1)
-        pl.semaphore_wait(entered.at[step, 1], 1)
+        @pl.when(z < 16 - (1 << step))
+        def _():
+            pl.semaphore_wait(entered.at[step, 0], 1)
+
+        @pl.when(z >= 1 << step)
+        def _():
+            pl.semaphore_wait(entered.at[step, 1], 1)
 
     greet(0)
     relay_staged(0)
@@ -285,12 +308,21 @@
     for n in range(1, NCH + 1):
         if n < NCH:
             relay_staged(n)
+        take_partner(n - 1)
+        relay_near(n - 1)
         relay_partner(n - 1)
-        relay_near(n - 1)
-        if n <= 3:
-            greeted(n - 1)
-            if n < 3:
-                greet(n)
+        if n == NCH:
+            for m in range(1, NCH):
+                far_wrap(m)
+        if n == 1:
+            greeted(0)
+            greet(1)
+        elif n == 2:
+            greeted(1)
+            greet(2)
+        elif n == NCH:
+            greeted(2)
+            greet(3)
         start = (n - 1) * CH
         split_far(0, start, CH)
         split_near(UP, start, CH)
@@ -310,9 +342,9 @@
         squares = folded(amp * amp)
         sums[5 + slot] = squares if slot == OWN else 2.0 * squares
 
+    before = jnp.where(q == 0, REST, SIB)
     swap = remote(
-        crossed.at[jnp.where(half == 0, jnp.where(q == 0, SIB, REST), UP)],
-        other_tile, x_send, x_recv, (jnp.where(half == 0, occ_at(1), up), v),
+        crossed.at[jnp.where(half == 0, DOWN, before)], other_tile, x_send, x_recv, (o, mate)
     )
     swap.start()
 
@@ -321,19 +353,16 @@
         [diag_weights(k_next[:, at * 128:(at + 1) * 128], slot) for at, slot in enumerate((UP, DOWN, REST))],
         axis=1,
     )
-    add_density(bars, near_h.at[256:640], near_l.at[256:640])
-    add_density(2.0 * crossed[OWN].T, far_h.at[0:ROWS], far_l.at[0:ROWS])
-
     def trace_one():
         swap.wait()
-        here = crossed[jnp.where(half == 0, jnp.where(q == 0, REST, SIB), DOWN)]
-        product = 2.0 * folded(here * other_tile[...])
-        before = jnp.where(q == 0, sums[REST] + sums[5 + REST], sums[SIB] + sums[5 + SIB])
-        before = before - jnp.where(half == 0, product, 0.0)
+        here = crossed[jnp.where(half == 0, before, DOWN)]
+        product = 2.0 * folded(here * other_tile[...].T)
+        first = jnp.where(q == 0, sums[REST] + sums[5 + REST], sums[SIB] + sums[5 + SIB])
+        first = first - jnp.where(half == 0, product, 0.0)
         second = sums[DOWN] + sums[5 + DOWN] - jnp.where(half == 0, 0.0, product)
         tile_out[...] = jnp.zeros((8, 128), F32)
         tile_out[0:1, :] = jnp.sum(sums[OWN] + sums[5 + OWN], axis=0, keepdims=True)
-        tile_out[1:2, :] = jnp.sum(before, axis=0, keepdims=True)
+        tile_out[1:2, :] = jnp.sum(first, axis=0, keepdims=True)
         tile_out[2:3, :] = jnp.sum(second, axis=0, keepdims=True)
         for copy in round_one:
             copy.start()
@@ -345,21 +374,22 @@
         for r in range(7):
             total = total + tile_in[r]
         next_out[...] = total
+        greeted(3)
         for copy in round_two:
             copy.start()
 
-    near_z = [(0, mate)] + [(d, side) for d in (1, 2, 3) for side in (v, mate)]
     round_one = [
-        remote(
-            tile_out, tile_in.at[k], t_send.at[k], t_recv.at[k],
-            (o, lax.rem(side + 2 * d, 32)),
-        )
-        for k, (d, side) in enumerate(near_z)
+        remote(tile_out, tile_in.at[r - 1], t_send.at[r - 1], t_recv.at[r - 1], (o, flipped(r)))
+        for r in range(1, 8)
     ]
     round_two = [
-        remote(next_out, next_in.at[k], t_send.at[7 + k], t_recv.at[7 + k], (o, vir_at(d)))
-        for k, d in enumerate((4, 8, -4))
+        remote(next_out, next_in.at[k], t_send.at[7 + k], t_recv.at[7 + k], (o, flipped(r)))
+        for k, r in enumerate((8, 16, 24))
     ]
+
+    trace_one()
+    add_density(bars, near_h.at[256:640], near_l.at[256:640])
+    add_density(2.0 * crossed[OWN].T, far_h.at[0:ROWS], far_l.at[0:ROWS])
 
     own_pair = near_rows(OWN)
     for n in range(NCH):
@@ -380,8 +410,6 @@
             bars.append(2.0 * amp - crossed[slot, pl.ds(start, CH), :])
         add_density(jnp.concatenate(bars, axis=0).T, far_h, far_l)
         if n == 0:
-            trace_one()
-        elif n == NCH - 2:
             trace_two()
 
     for copy in round_one:
@@ -421,7 +449,7 @@
     return pl.pallas_call(
         kernel,
         out_shape=(
-            jax.ShapeDtypeStruct((1,) + block, F32),
+            pltpu.VMEM((1,) + block, F32),
             jax.ShapeDtypeStruct((1, 3), F32),
         ),
         in_specs=[pl.BlockSpec(memory_space=pltpu.HBM), vmem, vmem],
@@ -455,7 +483,7 @@
             dma((10,)),
             dma,
             dma,
-            pltpu.SemaphoreType.REGULAR((3, 2)),
+            pltpu.SemaphoreType.REGULAR((4, 2)),
         ],
         compiler_params=pltpu.CompilerParams(
             collective_id=0, has_side_effects=True, vmem_limit_bytes=62 << 20

time: 70.3 us -> 61 us (0.87)
  Pallas kernels: 66.3 us -> 58.3 us
  local copies, waits for them, and re-layouts: 2.48 us -> 1.35 us
    pallas_call x1, Pallas kernels: 66.3 us -> 58.3 us  [local(): pl.pallas_call(kernel, out_shape=(pltpu.VMEM((1,) + block, F32), jax.Shap...]
    unnamed x4, local copies, waits for them, and re-layouts: 2.48 us -> 1.35 us
where the time goes in v3:
time: 61 us; the launch traced here: 60.9 us
  Pallas kernels  58.3 us (96%)
  local copies, waits for them, and re-layouts  1.35 us (2%)
  between operations  1.29 us (2%)
    pallas_call x1, Pallas kernels, local(): pl.pallas_call(kernel, out_shape=(pltpu.VMEM((1,) + block, F32), jax.Shap...  58.3 us
    unnamed x4, local copies, waits for them, and re-layouts  1.35 us

profile of v3, /device:TPU:1, one launch (start us, length us, event | category | flops | bytes accessed | tf_op | source)
XLA Modules:
  0.0 60.9 jit_solution(9364601549296162095)
XLA Ops:
  1.3 58.3 %shard_map.50 = (f32[1,128,1280]{2,1,0:T(8,128)S(1)}, f32[1,3]{1,0:T(1,128)}) custom-call(f32[1,128,1280]{2,1,0:T(8,128)} %factor.1, f32[1,1]{1,0:T(1,128)} %bitcast.2.occ, f32[1,128]{1,0:T(1,128)} %bitcast.3), custom_call_target="tpu_custom_call" | custom-call | flops 3019898880 | bytes 1310720 | tf_op jit(solution)/shard_map/pallas_call | solution.py:449
  59.5 0.0 copy-start
  59.5 0.8 %copy.7 = f32[1,128,1280]{2,1,0:T(8,128)} copy(f32[1,128,1280]{2,1,0:T(8,128)S(1)} %get-tuple-element.2) | data formatting | bytes 1310720
  60.4 0.0 copy-done
  60.4 0.5 copy.9
Async XLA Ops:
  59.5 0.9 %copy-start = (f32[1,3]{1,0:T(1,128)S(1)}, f32[1,3]{1,0:T(1,128)}, u32[]{:S(2)}) copy-start(f32[1,3]{1,0:T(1,128)} %get-tuple-element.7) | copy-start | bytes 40

commit v4 on v3

--- a/solution.py
+++ b/solution.py
@@ -43,7 +43,7 @@
 def kernel(
     factor, occ, vir, density, trace,
     own, near, far, staged, near_h, near_l, far_h, far_l, crossed, energy, energies, sums,
-    other_tile, tile_out, tile_in, next_out, next_in,
+    turned, other_tile, one_out, tile_in, next_out, next_in,
     own_sem, send_sem, near_sem, far_sem, staged_sem, e_send, e_recv, t_send, t_recv,
     x_send, x_recv, entered,
 ):
@@ -117,7 +117,7 @@
         return ref.at[pl.ds(n * CH, CH)]
 
     def mine(n):
-        return factor.at[0, pl.ds(n * CH, CH)]
+        return own.at[pl.ds(n * CH, CH)]
 
     def to_near(src, slot, n, flow, device):
         return remote(
@@ -157,6 +157,7 @@
         def _():
             to_far(mine(n), UP, n, S_FAR_DOWN, (down, mate)).start()
 
+    own_copy.wait()
     for n in range(NCH):
         @pl.when(edge)
         def _():
@@ -258,12 +259,12 @@
             row = jnp.where(q == 0, energies[0, 1:2, :], energies[1, 1:2, :])
         return row + energy[1:2, :]
 
-    def diag_weights(k_tile, slot):
+    def diag_weights(k_tile, slot, turned=False):
         across_b = jnp.broadcast_to(energy[0:1, :], (ROWS, 128))
         gap = pair_energy(slot) - across_b.T - across_b
         amp = k_tile / gap
-        bar = 2.0 * amp - amp.T
-        sums[slot] = folded(amp * bar)
+        bar = 2.0 * amp.T - amp if turned else 2.0 * amp - amp.T
+        sums[slot] = folded((amp.T if turned else amp) * bar)
         return 2.0 * bar if slot == OWN else bar
 
     def greet(step):
@@ -290,7 +291,6 @@
 
     greet(0)
     relay_staged(0)
-    own_copy.wait()
     h, l = halves(own[...])
     near_h[0:ROWS, :] = h
     near_l[0:ROWS, :] = l
@@ -305,70 +305,83 @@
     )
     add_density(bars, near_h.at[0:256], near_l.at[0:256], fresh=True)
 
+    far_row = jnp.broadcast_to(energies[4, 0:1, :], (ROWS, 128)).T
+    own_row = jnp.broadcast_to(energy[0:1, :], (ROWS, 128))
     for n in range(1, NCH + 1):
         if n < NCH:
             relay_staged(n)
         take_partner(n - 1)
         relay_near(n - 1)
         relay_partner(n - 1)
-        if n == NCH:
-            for m in range(1, NCH):
-                far_wrap(m)
         if n == 1:
             greeted(0)
             greet(1)
         elif n == 2:
             greeted(1)
             greet(2)
-        elif n == NCH:
+        elif n == 3:
             greeted(2)
             greet(3)
         start = (n - 1) * CH
         split_far(0, start, CH)
         split_near(UP, start, CH)
         split_near(DOWN, start, CH)
+        lot = [
+            jnp.concatenate(
+                [near[UP * ROWS + start:UP * ROWS + start + CH, :],
+                 near[DOWN * ROWS + start:DOWN * ROWS + start + CH, :],
+                 far[start:start + CH, :]],
+                axis=0,
+            )
+            for near, far in ((near_h, far_h), (near_l, far_l))
+        ]
+        k_lot = rows_dot(lot, near_rows(OWN, 2))
+        turned[0, start:start + CH, :] = k_lot[0:CH, :128]
+        turned[1, start:start + CH, :] = k_lot[CH:2 * CH, :128]
+        for slot in (OWN, SIB):
+            gap = pair_energy(slot) - far_row[start:start + CH, :] - own_row[0:CH, :]
+            crossed[slot, start:start + CH, :] = k_lot[2 * CH:, slot * 128:(slot + 1) * 128] / gap
 
     for n in range(NCH):
         wait_near(REST, n)
     split_near(REST, 0, ROWS)
 
-    far_row = jnp.broadcast_to(energies[4, 0:1, :], (ROWS, 128)).T
-    own_row = jnp.broadcast_to(energy[0:1, :], (ROWS, 128))
-    partner = (far_h[0:ROWS, :], far_l[0:ROWS, :])
-    k_cross = rows_dot(partner, near_rows(OWN, 5))
-    for slot in range(5):
-        amp = k_cross[:, slot * 128:(slot + 1) * 128] / (pair_energy(slot) - far_row - own_row)
-        crossed[slot] = amp
-        squares = folded(amp * amp)
-        sums[5 + slot] = squares if slot == OWN else 2.0 * squares
+    k_cross = rows_dot((far_h[0:ROWS, :], far_l[0:ROWS, :]), near_rows(UP, 3))
+    for at, slot in enumerate((UP, DOWN, REST)):
+        crossed[slot] = k_cross[:, at * 128:(at + 1) * 128] / (pair_energy(slot) - far_row - own_row)
 
     before = jnp.where(q == 0, REST, SIB)
     swap = remote(
         crossed.at[jnp.where(half == 0, DOWN, before)], other_tile, x_send, x_recv, (o, mate)
     )
     swap.start()
-
-    k_next = rows_dot(near_rows(OWN), near_rows(UP, 3))
+    for m in range(1, NCH):
+        far_wrap(m)
+    k_rest = rows_dot(near_rows(OWN), near_rows(REST))
     bars = jnp.concatenate(
-        [diag_weights(k_next[:, at * 128:(at + 1) * 128], slot) for at, slot in enumerate((UP, DOWN, REST))],
+        [
+            diag_weights(turned[0], UP, True),
+            diag_weights(turned[1], DOWN, True),
+            diag_weights(k_rest, REST),
+        ],
         axis=1,
     )
     def trace_one():
+        squares = [2.0 * folded(crossed[slot] * crossed[slot]) for slot in (before, DOWN)]
+        squares.insert(0, folded(crossed[OWN] * crossed[OWN]))
         swap.wait()
         here = crossed[jnp.where(half == 0, before, DOWN)]
         product = 2.0 * folded(here * other_tile[...].T)
-        first = jnp.where(q == 0, sums[REST] + sums[5 + REST], sums[SIB] + sums[5 + SIB])
-        first = first - jnp.where(half == 0, product, 0.0)
-        second = sums[DOWN] + sums[5 + DOWN] - jnp.where(half == 0, 0.0, product)
-        tile_out[...] = jnp.zeros((8, 128), F32)
-        tile_out[0:1, :] = jnp.sum(sums[OWN] + sums[5 + OWN], axis=0, keepdims=True)
-        tile_out[1:2, :] = jnp.sum(first, axis=0, keepdims=True)
-        tile_out[2:3, :] = jnp.sum(second, axis=0, keepdims=True)
+        squares[1] = squares[1] - jnp.where(half == 0, product, 0.0)
+        squares[2] = squares[2] - jnp.where(half == 0, 0.0, product)
+        one_out[...] = jnp.zeros((8, 128), F32)
+        for k, slot in enumerate((OWN, before, DOWN)):
+            one_out[k:k + 1, :] = jnp.sum(sums[slot] + squares[k], axis=0, keepdims=True)
         for copy in round_one:
             copy.start()
 
     def trace_two():
-        total = tile_out[...]
+        total = one_out[...]
         for copy in round_one:
             copy.wait_recv()
         for r in range(7):
@@ -379,8 +392,8 @@
             copy.start()
 
     round_one = [
-        remote(tile_out, tile_in.at[r - 1], t_send.at[r - 1], t_recv.at[r - 1], (o, flipped(r)))
-        for r in range(1, 8)
+        remote(one_out, tile_in.at[k], t_send.at[k], t_recv.at[k], (o, flipped(r)))
+        for k, r in enumerate(range(1, 8))
     ]
     round_two = [
         remote(next_out, next_in.at[k], t_send.at[7 + k], t_recv.at[7 + k], (o, flipped(r)))
@@ -388,12 +401,16 @@
     ]
 
     trace_one()
+    relay_far(0)
     add_density(bars, near_h.at[256:640], near_l.at[256:640])
     add_density(2.0 * crossed[OWN].T, far_h.at[0:ROWS], far_l.at[0:ROWS])
 
     own_pair = near_rows(OWN)
+    trace_two()
+    relay_far(1)
     for n in range(NCH):
-        relay_far(n)
+        if 1 < n + 1 < NCH:
+            relay_far(n + 1)
         start = n * CH
         wait_far(SIB, n)
         wait_far(REST, n)
@@ -409,8 +426,6 @@
             amp = k_tile[at * CH:(at + 1) * CH, :] / gap
             bars.append(2.0 * amp - crossed[slot, pl.ds(start, CH), :])
         add_density(jnp.concatenate(bars, axis=0).T, far_h, far_l)
-        if n == 0:
-            trace_two()
 
     for copy in round_one:
         copy.wait_send()
@@ -466,7 +481,8 @@
             pltpu.VMEM((5, ROWS, 128), F32),
             pltpu.VMEM((8, 128), F32),
             pltpu.VMEM((5, 8, 128), F32),
-            pltpu.VMEM((10, 8, 128), F32),
+            pltpu.VMEM((5, 8, 128), F32),
+            pltpu.VMEM((2, ROWS, 128), F32),
             pltpu.VMEM((ROWS, 128), F32),
             pltpu.VMEM((8, 128), F32),
             pltpu.VMEM((7, 8, 128), F32),

time: 61 us -> 61.2 us (level)
  the two profiles are of different devices: /device:TPU:1 before, /device:TPU:8 now
where the time goes in v4:
time: 61.2 us; the launch traced here: 61 us
  Pallas kernels  58.4 us (95%)
  local copies, waits for them, and re-layouts  1.35 us (2%)
  between operations  1.29 us (2%)
    pallas_call x1, Pallas kernels, local(): pl.pallas_call(kernel, out_shape=(pltpu.VMEM((1,) + block, F32), jax.Shap...  58.4 us
    unnamed x4, local copies, waits for them, and re-layouts  1.35 us

profile of v4, /device:TPU:8, one launch (start us, length us, event | category | flops | bytes accessed | tf_op | source)
XLA Modules:
  0.0 61.0 jit_solution(9572131237497301782)
XLA Ops:
  1.3 58.4 %shard_map.50 = (f32[1,128,1280]{2,1,0:T(8,128)S(1)}, f32[1,3]{1,0:T(1,128)}) custom-call(f32[1,128,1280]{2,1,0:T(8,128)} %factor.1, f32[1,1]{1,0:T(1,128)} %bitcast.2.occ, f32[1,128]{1,0:T(1,128)} %bitcast.3), custom_call_target="tpu_custom_call" | custom-call | flops 3019898880 | bytes 1310720 | tf_op jit(solution)/shard_map/pallas_call | solution.py:464
  59.6 0.0 copy-start
  59.6 0.8 %copy.7 = f32[1,128,1280]{2,1,0:T(8,128)} copy(f32[1,128,1280]{2,1,0:T(8,128)S(1)} %get-tuple-element.2) | data formatting | bytes 1310720
  60.5 0.0 copy-done
  60.5 0.5 copy.9
Async XLA Ops:
  59.6 0.9 %copy-start = (f32[1,3]{1,0:T(1,128)S(1)}, f32[1,3]{1,0:T(1,128)}, u32[]{:S(2)}) copy-start(f32[1,3]{1,0:T(1,128)} %get-tuple-element.7) | copy-start | bytes 40

commit v5 on v4

--- a/solution.py
+++ b/solution.py
@@ -400,9 +400,9 @@
         for k, r in enumerate((8, 16, 24))
     ]
 
+    add_density(bars, near_h.at[256:640], near_l.at[256:640])
     trace_one()
     relay_far(0)
-    add_density(bars, near_h.at[256:640], near_l.at[256:640])
     add_density(2.0 * crossed[OWN].T, far_h.at[0:ROWS], far_l.at[0:ROWS])
 
     own_pair = near_rows(OWN)
@@ -465,7 +465,7 @@
         kernel,
         out_shape=(
             pltpu.VMEM((1,) + block, F32),
-            jax.ShapeDtypeStruct((1, 3), F32),
+            pltpu.VMEM((1, 3), F32),
         ),
         in_specs=[pl.BlockSpec(memory_space=pltpu.HBM), vmem, vmem],
         out_specs=(vmem, vmem),

time: 61.2 us -> 60.6 us (level)
    unnamed x4 -> x2, local copies, waits for them, and re-layouts: 1.35 us -> 1.35 us
where the time goes in v5:
time: 60.6 us; the launch traced here: 60.4 us
  Pallas kernels  57.8 us (95%)
  local copies, waits for them, and re-layouts  1.35 us (2%)
  between operations  1.28 us (2%)
    pallas_call x1, Pallas kernels, local(): pl.pallas_call(kernel, out_shape=(pltpu.VMEM((1,) + block, F32), pltpu.VM...  57.8 us
    unnamed x2, local copies, waits for them, and re-layouts  1.35 us

profile of v5, /device:TPU:8, one launch (start us, length us, event | category | flops | bytes accessed | tf_op | source)
XLA Modules:
  0.0 60.4 jit_solution(7098583864924728408)
XLA Ops:
  1.3 57.8 %shard_map.50 = (f32[1,128,1280]{2,1,0:T(8,128)S(1)}, f32[1,3]{1,0:T(1,128)S(1)}) custom-call(f32[1,128,1280]{2,1,0:T(8,128)} %factor.1, f32[1,1]{1,0:T(1,128)} %bitcast.2.occ, f32[1,128]{1,0:T(1,128)} %bitcast.3), custom_call_target="tpu_custom_call" | custom-call | flops 3019898880 | bytes 1310720 | tf_op jit(solution)/shard_map/pallas_call | solution.py:464
  59.1 0.8 %copy.7 = f32[1,128,1280]{2,1,0:T(8,128)} copy(f32[1,128,1280]{2,1,0:T(8,128)S(1)} %get-tuple-element.2) | data formatting | bytes 1310720
  59.9 0.5 copy.8
